TPU v7x, 32 devices: a whole 2x2x4 slice. The times are simulated.
32 devices in a mesh: rows: 4 (over y, core), cols: 8 (over z, x).
Axes of the slice: x: 2, y: 2, z: 4, core: 2. Of those that a mesh axis runs over, the one named last changes fastest.
Arguments:
- displacement: float32 [2048, 288], P(('rows', 'cols')), may hold values from -6 to 6
- positions: float32 [2048, 288], P(('rows', 'cols')), as said below
- cluster_basis: bfloat16 [2048, 288, 64], P(('rows', 'cols')), may hold values from -0.375 to 0.375
- near_pairs: int32 [8192, 2], P(('rows', 'cols')), may hold values from 0 to 67, as said below
- near_count: int32 [32], P(('rows', 'cols')), may hold values from 64 to 256, as said below
- far_pairs: int32 [32768, 2], P(('rows', 'cols')), may hold values from 0 to 511, as said below
- far_count: int32 [32], P(('rows', 'cols')), may hold values from 256 to 1024, as said below
- far_blocks: bfloat16 [32768, 64, 64], P(('rows', 'cols')), may hold values from -0.75 to 0.75
- intact: int32 [2048, 96], P(('rows', 'cols')), may hold values 0 or 1
- stiffness: float32 [2048, 96], P(('rows', 'cols')), may hold values from 0.5 to 2
Outputs:
- net_traction: float32 [2048, 288], P(('rows', 'cols'))
- damage: float32 [2048, 96], P(('rows', 'cols'))
Inputs may be any that keep to these rules, and one draw needn't show every extreme that they name: `positions`: centroids of the elements of each cluster. `near_pairs`: column 0 is a cluster of the device's own 64; column 1 counts from 2 clusters before the device's first cluster and names a cluster at most 2 away from the target in the cluster order. Dead slots hold valid entries too. `near_count`: loads differ from device to device. `far_pairs`: column 0 is a target cluster of the device's index along rows (0 to 511); column 1 a source cluster of its index along cols (0 to 255), numbered through the devices of that column in the order of rows. Dead slots hold valid entries too. `far_count`: loads differ from device to device.
All inputs are finite; a program needn't handle non-finite values. No bound on the sum of `intact` on one device may be relied on, other than what follows from the above.
Results may differ from a plain program's by a relative error of at most 0.0014.
Values may be sent and summed in bfloat16 or wider, within the bound.
No kernel may reach another device: no remote copies, remote signals or barrier semaphores. Data moves between devices by JAX's collectives and lax.ppermute only.
A program may use at most 128 MiB of HBM per device.

v0:
```python
import functools

import jax
import jax.numpy as jnp
from jax import lax
from jax.experimental import pallas as pl
from jax.experimental.pallas import tpu as pltpu
from jax.sharding import PartitionSpec as P

HALO = 2
LANES = 128
SUBLANES = 8
CHUNK = 32
GROUPS = LANES // CHUNK
core_square = 0.25
softening = 1.5
UNROLL = 8
TOGETHER = 2
FEW = 4
FOLD = 256
PIECES = 3
VMEM = 20 * 1024 * 1024


def split_rows(width, lanes):
    return pl.cdiv(width, lanes)


def in_hbm(count):
    return [pl.BlockSpec(memory_space=pltpu.HBM)] * count


def pinned(*arrays):
    return [pltpu.with_memory_space_constraint(x, pltpu.HBM) for x in arrays]


def start_all(sems, moves):
    copies = [
        pltpu.make_async_copy(source, target, sems.at[n])
        for n, (source, target) in enumerate(moves)
    ]
    for copy in copies:
        copy.start()
    return copies


def prepare_kernel(
    near_count_ref,
    far_count_ref,
    disp_hbm,
    pos_hbm,
    low_ref,
    halo_ref,
    counts_ref,
    disp_ref,
    pos_ref,
    sems,
):
    clusters, width = disp_ref.shape
    spare = halo_ref.shape[1]
    segments = split_rows(width, spare)
    inputs = start_all(sems, ((disp_hbm, disp_ref), (pos_hbm, pos_ref)))
    halo_ref[...] = jnp.zeros_like(halo_ref)
    row = lax.broadcasted_iota(jnp.int32, counts_ref.shape, 0)
    counts_ref[...] = jnp.where(row == 0, near_count_ref[0], far_count_ref[0])
    for copy in inputs:
        copy.wait()
    low_ref[...] = disp_ref[...].astype(low_ref.dtype)
    row = 0
    for g in range(segments):
        size = min(spare, width - g * spare)
        for start in (0, clusters - HALO):
            for ref in (disp_ref, pos_ref):
                halo_ref[row : row + HALO, 0:size] = ref[
                    start : start + HALO, g * spare : g * spare + size
                ]
                row += HALO


def list_pairs(pairs_ref, near_count, list_ref, clusters):
    slots = pairs_ref.shape[1]
    target = pairs_ref[0:1, :]
    source = pairs_ref[1:2, :]
    slot = lax.broadcasted_iota(jnp.int32, (1, slots), 1)
    live = slot < near_count
    own = jnp.logical_and(source >= HALO, source < clusters + HALO)
    square = (slots, slots)
    first = lax.broadcasted_iota(jnp.int32, square, 0)
    upto = first <= lax.broadcasted_iota(jnp.int32, square, 1)
    upto = jnp.where(upto, 1.0, 0.0).astype(jnp.bfloat16)
    row = lax.broadcasted_iota(jnp.int32, (SUBLANES, slots), 0)
    pairs = jnp.where(row == 0, target, source).astype(jnp.float32).astype(jnp.bfloat16)
    results = []
    for wanted in (own, jnp.logical_not(own)):
        chosen = jnp.where(jnp.logical_and(live, wanted), 1.0, 0.0)
        order = jnp.dot(
            jnp.broadcast_to(chosen, (SUBLANES, slots)).astype(jnp.bfloat16),
            upto,
            preferred_element_type=jnp.float32,
        )
        place = first == jnp.where(chosen > 0.0, order[0:1, :] - 1.0, -1.0).astype(jnp.int32)
        place = jnp.where(place, 1.0, 0.0).astype(jnp.bfloat16)
        together = lax.dot_general(
            pairs, place, (((1,), (1,)), ((), ())), preferred_element_type=jnp.float32
        ).astype(jnp.int32)
        number = jnp.sum(chosen, axis=1, keepdims=True).astype(jnp.int32)
        results.append((together, jnp.broadcast_to(number, (1, slots))))
    (pairs, number), (others, others_number) = results
    list_ref[0:1, :] = pairs[0:1, :]
    list_ref[1:2, :] = jnp.clip(pairs[1:2, :] - HALO, 0, clusters - 1)
    list_ref[2:3, :] = jnp.where(slot < number, pairs[0:1, :], clusters) * SUBLANES
    list_ref[3:4, :] = number
    list_ref[4:6, :] = others[0:2, :]
    list_ref[6:7, :] = others_number
    list_ref[7:8, :] = jnp.zeros((1, slots), jnp.int32)


def prepare(near_count, far_count, disp, pos, spare):
    clusters, width = disp.shape
    vmem = pl.BlockSpec(memory_space=pltpu.VMEM)
    smem = pl.BlockSpec(memory_space=pltpu.SMEM)
    return pl.pallas_call(
        prepare_kernel,
        out_shape=(
            jax.ShapeDtypeStruct((clusters, width), jnp.bfloat16),
            jax.ShapeDtypeStruct((clusters, spare), jnp.float32),
            jax.ShapeDtypeStruct((SUBLANES, LANES), jnp.int32),
        ),
        in_specs=[smem] * 2 + in_hbm(2),
        out_specs=(vmem,) * 3,
        scratch_shapes=[
            pltpu.VMEM(disp.shape, disp.dtype),
            pltpu.VMEM(pos.shape, pos.dtype),
            pltpu.SemaphoreType.DMA((2,)),
        ],
        compiler_params=pltpu.CompilerParams(vmem_limit_bytes=VMEM),
        cost_estimate=pl.CostEstimate(
            flops=clusters * width, bytes_accessed=12 * clusters * width, transcendentals=0
        ),
        name="prepare",
    )(near_count, far_count, *pinned(disp, pos))


def far_kernel(
    counts_hbm,
    pairs_hbm,
    gathered_hbm,
    near_pairs_hbm,
    pos_hbm,
    disp_hbm,
    intact_hbm,
    stiff_hbm,
    blocks_ref,
    out_ref,
    pos_ref,
    hold_ref,
    list_ref,
    damage_hbm,
    counts_ref,
    pairs_ref,
    gathered_ref,
    near_pairs_ref,
    disp_ref,
    intact_ref,
    stiff_ref,
    damage_ref,
    buffer,
    column_scr,
    coeff_scr,
    place_scr,
    sum_scr,
    summed_scr,
    halo_scr,
    sems,
    block_sems,
    out_sem,
    *,
    segments,
):
    rank, _, slots = buffer.shape
    cols, clusters, _ = out_ref.shape
    targets = cols * clusters
    rows = gathered_ref.shape[0] // clusters
    sources = rows * clusters

    def fetch(t):
        here = pl.ds(pl.multiple_of(t * FOLD, FOLD), FOLD)
        return pltpu.make_async_copy(
            blocks_ref.at[:, :, here], buffer.at[:, :, here], block_sems.at[t]
        )

    inputs = start_all(
        sems,
        (
            (counts_hbm, counts_ref),
            (pairs_hbm, pairs_ref),
            (gathered_hbm, gathered_ref),
            (near_pairs_hbm, near_pairs_ref),
            (pos_hbm, pos_ref),
            (disp_hbm, disp_ref),
            (intact_hbm, intact_ref),
            (stiff_hbm, stiff_ref),
        ),
    )
    fetch(0).start()
    summed_scr[...] = jnp.zeros_like(summed_scr)
    inputs[0].wait()
    count = counts_ref[1, 0]
    live = (count + FOLD - 1) // FOLD

    @pl.when(live > 1)
    def _():
        fetch(1).start()

    inputs[1].wait()
    inputs[2].wait()
    column_scr[...] = gathered_ref[...].astype(jnp.bfloat16)

    index = lax.broadcasted_iota(jnp.int32, (sources, slots), 0)
    pick = jnp.where(index == pairs_ref[1:2, :], 1.0, 0.0).astype(jnp.bfloat16)
    coeff = lax.dot_general(
        column_scr[...], pick, (((0,), (0,)), ((), ())), preferred_element_type=jnp.float32
    )
    coeff_scr[...] = coeff[0:rank, :]
    slot = lax.broadcasted_iota(jnp.int32, (1, slots), 1)
    wanted = jnp.where(slot < count, pairs_ref[0:1, :], -1)
    index = lax.broadcasted_iota(jnp.int32, (targets, slots), 0)
    place_scr[...] = jnp.where(index == wanted, 1.0, 0.0).astype(jnp.bfloat16)

    for copy in inputs[3:]:
        copy.wait()
    list_pairs(near_pairs_ref, counts_ref[0, 0], list_ref, clusters)
    elems = damage_ref.shape[1]
    disp = [disp_ref[:, c * elems : (c + 1) * elems] for c in range(3)]
    separation = jnp.sqrt(1.0 + (disp[0] * disp[0] + disp[1] * disp[1] + disp[2] * disp[2]))
    softened = 1.0 - jnp.exp(-(separation - 1.0) / softening)
    intact = intact_ref[...].astype(jnp.float32)
    damage = intact * softened + (1.0 - intact)
    damage_ref[...] = damage
    damage_out = pltpu.make_async_copy(damage_ref, damage_hbm, out_sem)
    damage_out.start()
    hold_ref[...] = (1.0 - damage) * stiff_ref[...]

    def multiply(t, carry):
        start = pl.multiple_of(t * FOLD, FOLD)
        lanes = pl.ds(start, FOLD)
        fetch(t).wait()

        @pl.when(t + 2 < live)
        def _():
            fetch(t + 2).start()

        coeff = coeff_scr[:, lanes]
        for r in range(rank):
            product = buffer[r, :, lanes].astype(jnp.float32) * coeff
            folded = product[0:SUBLANES]
            for s in range(1, rank // SUBLANES):
                folded = folded + product[s * SUBLANES : (s + 1) * SUBLANES]
            for h in range(FOLD // LANES):
                sum_scr[h, r * SUBLANES : (r + 1) * SUBLANES, :] = folded[
                    :, h * LANES : (h + 1) * LANES
                ]
        parts = []
        for h in range(FOLD // LANES):
            total = sum_scr[h, pl.ds(0, rank, stride=SUBLANES), :]
            for s in range(1, SUBLANES):
                total = total + sum_scr[h, pl.ds(s, rank, stride=SUBLANES), :]
            parts.append(total)
        coupled = jnp.concatenate(parts, axis=1)
        high = coupled.astype(jnp.bfloat16)
        low = (coupled - high.astype(jnp.float32)).astype(jnp.bfloat16)
        both = jnp.concatenate([high, low], axis=0)
        summed_scr[...] += lax.dot_general(
            place_scr[:, lanes], both, (((1,), (1,)), ((), ())), preferred_element_type=jnp.float32
        )
        return carry

    lax.fori_loop(0, live, multiply, 0)
    damage_out.wait()

    i = lax.axis_index("rows")
    j = lax.axis_index("cols")
    from_last = jnp.where(j < cols - 1, i, i - 1)
    from_first = jnp.where(j > 0, i, i + 1)
    edge = 2 * HALO
    halo_scr[...] = jnp.zeros_like(halo_scr)
    sides = (
        (0, jnp.minimum(from_first, rows - 1), from_first < rows),
        (edge, jnp.maximum(from_last, 0), from_last >= 0),
    )
    for side, (row, owner, there) in enumerate(sides):
        start = pl.multiple_of(owner * clusters, clusters)
        whole = jnp.where(there, gathered_ref[pl.ds(start, clusters), :], 0.0)
        for n in range(PIECES):
            piece = whole.astype(jnp.bfloat16).astype(jnp.float32)
            whole = whole - piece
            for g in range(segments):
                to = (n * segments + g) * edge
                here = g * 2 * edge + row
                halo_scr[side, to : to + edge, :] = piece[here : here + edge, :]
    after = jnp.where(j < cols - 1, j + 1, 0)
    lane = lax.broadcasted_iota(jnp.int32, (clusters, LANES), 1)
    for d in range(cols):
        halo = halo_scr[jnp.where(after == d, 1, 0)]
        mine = summed_scr[d * clusters : (d + 1) * clusters, :]
        mine = mine + pltpu.roll(mine, rank, 1)
        out_ref[d] = jnp.where(lane < rank, mine, halo).astype(out_ref.dtype)


def far_field(
    counts, pairs, gathered, near_pairs, pos, disp, intact, stiffness, blocks, cols, segments
):
    rank, _, slots = blocks.shape
    rows = lax.axis_size("rows")
    clusters = gathered.shape[0] // rows
    return pl.pallas_call(
        functools.partial(far_kernel, segments=segments),
        out_shape=(
            jax.ShapeDtypeStruct((cols, clusters, LANES), jnp.bfloat16),
            jax.ShapeDtypeStruct(pos.shape, jnp.float32),
            jax.ShapeDtypeStruct(stiffness.shape, jnp.float32),
            jax.ShapeDtypeStruct((SUBLANES, near_pairs.shape[1]), jnp.int32),
            jax.ShapeDtypeStruct(stiffness.shape, jnp.float32),
        ),
        in_specs=in_hbm(9),
        out_specs=(pl.BlockSpec(memory_space=pltpu.VMEM),) * 4 + tuple(in_hbm(1)),
        scratch_shapes=[
            pltpu.SMEM(counts.shape, counts.dtype),
            pltpu.VMEM(pairs.shape, pairs.dtype),
            pltpu.VMEM(gathered.shape, gathered.dtype),
            pltpu.VMEM(near_pairs.shape, near_pairs.dtype),
            pltpu.VMEM(disp.shape, disp.dtype),
            pltpu.VMEM(intact.shape, intact.dtype),
            pltpu.VMEM(stiffness.shape, stiffness.dtype),
            pltpu.VMEM(stiffness.shape, jnp.float32),
            pltpu.VMEM(blocks.shape, blocks.dtype),
            pltpu.VMEM((rows * clusters, LANES), jnp.bfloat16),
            pltpu.VMEM((rank, slots), jnp.float32),
            pltpu.VMEM((cols * clusters, slots), jnp.bfloat16),
            pltpu.VMEM((FOLD // LANES, rank * SUBLANES, LANES), jnp.float32),
            pltpu.VMEM((cols * clusters, LANES), jnp.float32),
            pltpu.VMEM((2, clusters, LANES), jnp.float32),
            pltpu.SemaphoreType.DMA((8,)),
            pltpu.SemaphoreType.DMA((slots // FOLD,)),
            pltpu.SemaphoreType.DMA(()),
        ],
        compiler_params=pltpu.CompilerParams(vmem_limit_bytes=VMEM),
        cost_estimate=pl.CostEstimate(
            flops=2 * rank * rank * slots,
            bytes_accessed=2 * rank * rank * slots,
            transcendentals=0,
        ),
        name="far_field",
    )(
        counts,
        *pinned(pairs),
        gathered,
        *pinned(near_pairs, pos, disp, intact, stiffness, blocks),
    )


def replicate(rows, chunks, store, turned=False):
    within = lax.broadcasted_iota(jnp.int32, (rows.shape[0], LANES), 1)
    if turned:
        within = within + (within // CHUNK) * SUBLANES
    within = within % CHUNK
    for m in range(3 * chunks):
        tile = m // GROUPS
        store(
            m,
            jnp.take_along_axis(
                rows[:, tile * LANES : (tile + 1) * LANES],
                within + (m % GROUPS) * CHUNK,
                axis=1,
                mode="promise_in_bounds",
            ),
        )


def row_of(ref, n, row):
    return ref[n, pl.ds(row, SUBLANES, stride=0), :]


def turn(wide):
    return pltpu.roll(wide, 0, 1, stride=1, stride_axis=0)


def pair_sums(tgt, src, chunks):
    sums = [None] * (3 * chunks)
    size = 3 * chunks
    for h in range(chunks):
        x = [tgt(c * chunks + h) for c in range(3)]
        for f in range(chunks):
            r = [x[c] - src(c * chunks + f) for c in range(3)]
            u = [src(size + c * chunks + f) for c in range(3)]
            q = (r[0] * r[0] + core_square) + (r[1] * r[1] + r[2] * r[2])
            s = r[0] * u[0] + (r[1] * u[1] + r[2] * u[2])
            inverse = lax.rsqrt(q)
            square = inverse * inverse
            weight = square * inverse
            s = (3.0 * s) * square
            for c in range(3):
                term = weight * (u[c] - s * r[c])
                m = c * chunks + h
                sums[m] = term if sums[m] is None else sums[m] + term
    return sums


def gather_sums(acc_scr, clusters, chunks, store):
    own_group = lax.broadcasted_iota(jnp.int32, (clusters, LANES), 1) // CHUNK
    for t in range(pl.cdiv(3 * chunks, GROUPS)):
        merged = None
        for g in range(GROUPS):
            m = t * GROUPS + g
            if m >= 3 * chunks:
                break
            total = acc_scr[m, pl.ds(0, clusters, stride=SUBLANES), :]
            for s in range(1, SUBLANES):
                total = total + acc_scr[m, pl.ds(s, clusters, stride=SUBLANES), :]
            total = total + pltpu.roll(total, 2 * CHUNK, 1)
            total = total + pltpu.roll(total, CHUNK, 1)
            merged = total if merged is None else jnp.where(own_group == g, total, merged)
        store(t, merged)


def turn_matrix():
    shape = (PIECES * CHUNK, SUBLANES * LANES)
    column = lax.broadcasted_iota(jnp.int32, shape, 1)
    lane = column % LANES
    entry = (lane + (lane // CHUNK) * SUBLANES + column // LANES) % CHUNK
    row = lax.broadcasted_iota(jnp.int32, shape, 0) % CHUNK
    return jnp.where(entry == row, 1.0, 0.0).astype(jnp.bfloat16)


def exact_pieces(value):
    pieces = []
    for _ in range(PIECES):
        piece = value.astype(jnp.bfloat16)
        pieces.append(piece)
        value = value - piece.astype(jnp.float32)
    return pieces


def near_kernel(
    list_hbm,
    disp_hbm,
    pos_ref,
    hold_ref,
    out_ref,
    edge_ref,
    list_ref,
    disp_ref,
    wide_scr,
    piece_scr,
    turn_scr,
    tgt_scr,
    src_scr,
    acc_scr,
    sems,
):
    clusters, width = pos_ref.shape
    elems = width // 3
    chunks = elems // CHUNK
    size = 3 * chunks

    moves = start_all(sems, ((list_hbm, list_ref), (disp_hbm, disp_ref)))
    acc_scr[...] = jnp.zeros_like(acc_scr)
    turn_scr[...] = turn_matrix()

    wide_scr[:, 0:width] = pos_ref[...]
    edge_ref[0:HALO, :] = pos_ref[0:HALO, :]
    edge_ref[HALO:, :] = pos_ref[clusters - HALO :, :]
    columns = 2 * LANES
    for k, values in enumerate((pos_ref, disp_ref)):
        if k == 1:
            moves[1].wait()
        for m in range(size):
            pieces = exact_pieces(values[:, m * CHUNK : (m + 1) * CHUNK])
            piece_scr[m * clusters : (m + 1) * clusters, :] = jnp.concatenate(pieces, axis=1)
        for t in range(SUBLANES * LANES // columns):
            turned = jnp.dot(
                piece_scr[...],
                turn_scr[:, t * columns : (t + 1) * columns],
                preferred_element_type=jnp.float32,
            )
            for m in range(size):
                for h in range(columns // LANES):
                    s = t * (columns // LANES) + h
                    src_scr[k * size + m, pl.ds(s, clusters, stride=SUBLANES), :] = turned[
                        m * clusters : (m + 1) * clusters, h * LANES : (h + 1) * LANES
                    ]

    def store_target(m, value):
        tgt_scr[m] = value

    replicate(wide_scr[...], chunks, store_target)
    moves[0].wait()
    count = list_ref[3, 0]

    def sums_of(slot):
        target = list_ref[0, slot]
        source = pl.multiple_of(list_ref[1, slot] * SUBLANES, SUBLANES)
        return pair_sums(
            lambda m: row_of(tgt_scr, m, target),
            lambda n: src_scr[n, pl.ds(source, SUBLANES), :],
            chunks,
        )

    def step(it, carry):
        for k in range(0, UNROLL, TOGETHER):
            slots = [it * UNROLL + k + n for n in range(TOGETHER)]
            results = [sums_of(slot) for slot in slots]
            for slot, sums in zip(slots, results):
                into = pl.multiple_of(list_ref[2, slot], SUBLANES)
                for m in range(size):
                    acc_scr[m, pl.ds(into, SUBLANES), :] += sums[m]
        return carry

    lax.fori_loop(0, (count + UNROLL - 1) // UNROLL, step, 0)

    def store_sum(t, value):
        wide_scr[:, t * LANES : (t + 1) * LANES] = value

    gather_sums(acc_scr, clusters, chunks, store_sum)
    for c in range(3):
        here = slice(c * elems, (c + 1) * elems)
        out_ref[:, here] = wide_scr[:, here] - hold_ref[...] * disp_ref[:, here]


def near_field(listed, disp, pos, hold):
    clusters, width = pos.shape
    elems = width // 3
    chunks = elems // CHUNK
    padded = pl.cdiv(width, LANES) * LANES
    slots = listed.shape[1]
    vmem = pl.BlockSpec(memory_space=pltpu.VMEM)
    return pl.pallas_call(
        near_kernel,
        out_shape=(
            jax.ShapeDtypeStruct((clusters, width), jnp.float32),
            jax.ShapeDtypeStruct((2 * HALO, width), jnp.float32),
        ),
        in_specs=in_hbm(2) + [vmem] * 2,
        out_specs=(vmem, vmem),
        scratch_shapes=[
            pltpu.SMEM(listed.shape, listed.dtype),
            pltpu.VMEM(disp.shape, disp.dtype),
            pltpu.VMEM((clusters, padded), jnp.float32),
            pltpu.VMEM((3 * chunks * clusters, PIECES * CHUNK), jnp.bfloat16),
            pltpu.VMEM((PIECES * CHUNK, SUBLANES * LANES), jnp.bfloat16),
            pltpu.VMEM((3 * chunks, clusters, LANES), jnp.float32),
            pltpu.VMEM((6 * chunks, clusters * SUBLANES, LANES), jnp.float32),
            pltpu.VMEM((3 * chunks, (clusters + 1) * SUBLANES, LANES), jnp.float32),
            pltpu.SemaphoreType.DMA((2,)),
        ],
        compiler_params=pltpu.CompilerParams(vmem_limit_bytes=VMEM),
        cost_estimate=pl.CostEstimate(
            flops=30 * slots * elems * elems,
            bytes_accessed=4 * clusters * width * 6,
            transcendentals=slots * elems * elems,
        ),
        name="near_field",
    )(listed, *pinned(disp), pos, hold)


def finish_kernel(
    rest_hbm,
    edge_ref,
    received_ref,
    near_ref,
    far_ref,
    out_ref,
    rest_ref,
    ext_scr,
    halo_scr,
    tgt_scr,
    src_scr,
    acc_scr,
    sem,
    *,
    rank,
):
    clusters, width = near_ref.shape
    cols = received_ref.shape[0]
    elems = width // 3
    chunks = elems // CHUNK
    size = 3 * chunks
    spare = LANES - rank
    segments = split_rows(width, spare)
    edge = 2 * HALO

    fetch = pltpu.make_async_copy(rest_hbm, rest_ref, sem)
    fetch.start()
    acc_scr[...] = jnp.zeros_like(acc_scr)

    j = lax.axis_index("cols")
    before = jnp.where(j > 0, j - 1, cols - 1)
    after = jnp.where(j < cols - 1, j + 1, 0)
    for start, sender in ((0, before), (HALO, after)):
        halo_scr[...] = received_ref[sender].astype(jnp.float32)
        rows = edge * segments
        whole = halo_scr[0:rows, :]
        for n in range(1, PIECES):
            whole = whole + halo_scr[n * rows : (n + 1) * rows, :]
        for g in range(segments):
            count = min(spare, width - g * spare)
            for k in range(2):
                row = (2 * g + k) * HALO
                ext_scr[k, start : start + HALO, g * spare : g * spare + count] = whole[
                    row : row + HALO, rank : rank + count
                ]
    ext_scr[1, edge : 2 * edge, 0:width] = edge_ref[...]
    for k in range(2):

        def store(m, value, k=k):
            for b in range(edge):
                wide = jnp.broadcast_to(value[b : b + 1, :], (SUBLANES, LANES))
                src_scr[(1 - k) * size + m, b * SUBLANES : (b + 1) * SUBLANES, :] = turn(wide)

        replicate(ext_scr[k], chunks, store, True)

    def store_target(m, value):
        tgt_scr[m] = value

    replicate(ext_scr[1], chunks, store_target)
    fetch.wait()
    number = rest_ref[6, 0]

    def one_pair(n):
        target = rest_ref[4, n]
        source = rest_ref[5, n]
        target = jnp.where(target < HALO, target, target - (clusters - edge))
        source = jnp.where(source < HALO, source, source - clusters)
        live = n < number
        target = jnp.where(live, target, edge)
        source = pl.multiple_of(jnp.where(live, source, 0) * SUBLANES, SUBLANES)
        into = pl.multiple_of(target * SUBLANES, SUBLANES)
        row = edge + jnp.where(live, target, 0)
        sums = pair_sums(
            lambda m: row_of(tgt_scr, m, row),
            lambda k: src_scr[k, pl.ds(source, SUBLANES), :],
            chunks,
        )
        for m in range(size):
            acc_scr[m, pl.ds(into, SUBLANES), :] += sums[m]

    def step(it, carry):
        for k in range(FEW):
            one_pair(it * FEW + k)
        return carry

    lax.fori_loop(0, (number + FEW - 1) // FEW, step, 0)

    def store_sum(t, value):
        ext_scr[0, :, t * LANES : (t + 1) * LANES] = value

    gather_sums(acc_scr, 2 * edge, chunks, store_sum)
    out_ref[...] = near_ref[...] + far_ref[...]
    out_ref[0:HALO, :] += ext_scr[0, 0:HALO, 0:width]
    out_ref[clusters - HALO :, :] += ext_scr[0, HALO:edge, 0:width]


def finish(rest, edges, received, near, far, rank):
    clusters, width = near.shape
    chunks = width // 3 // CHUNK
    padded = pl.cdiv(width, LANES) * LANES
    edge = 2 * HALO
    vmem = pl.BlockSpec(memory_space=pltpu.VMEM)
    return pl.pallas_call(
        functools.partial(finish_kernel, rank=rank),
        out_shape=jax.ShapeDtypeStruct((clusters, width), jnp.float32),
        in_specs=in_hbm(1) + [vmem] * 4,
        out_specs=vmem,
        scratch_shapes=[
            pltpu.SMEM(rest.shape, rest.dtype),
            pltpu.VMEM((2, 2 * edge, padded), jnp.float32),
            pltpu.VMEM((clusters, LANES), jnp.float32),
            pltpu.VMEM((3 * chunks, 2 * edge, LANES), jnp.float32),
            pltpu.VMEM((6 * chunks, edge * SUBLANES, LANES), jnp.float32),
            pltpu.VMEM((3 * chunks, 2 * edge * SUBLANES, LANES), jnp.float32),
            pltpu.SemaphoreType.DMA(()),
        ],
        compiler_params=pltpu.CompilerParams(vmem_limit_bytes=VMEM),
        cost_estimate=pl.CostEstimate(
            flops=2 * clusters * width, bytes_accessed=16 * clusters * width, transcendentals=0
        ),
        name="finish",
    )(rest, edges, received, near, far)


def local(
    displacement,
    positions,
    cluster_basis,
    near_pairs,
    near_count,
    far_pairs,
    far_count,
    far_blocks,
    intact,
    stiffness,
):
    cols = lax.axis_size("cols")
    clusters, width, rank = cluster_basis.shape
    spare = LANES - rank
    segments = split_rows(width, spare)
    disp_bf, halo, counts = prepare(near_count, far_count, displacement, positions, spare)
    coeff = jnp.einsum("kf,kfr->kr", disp_bf, cluster_basis, preferred_element_type=jnp.float32)
    payload = jnp.concatenate([coeff, halo], axis=1)
    gathered = lax.all_gather(payload, "rows", axis=0, tiled=True)
    partial, pos, hold, listed, damage = far_field(
        counts,
        far_pairs.T,
        gathered,
        near_pairs.T,
        positions,
        displacement,
        intact,
        stiffness,
        far_blocks.transpose(1, 2, 0),
        cols,
        segments,
    )
    received = lax.all_to_all(partial, "cols", split_axis=0, concat_axis=0)
    near, edges = near_field(listed, displacement, pos, hold)
    owned = jnp.sum(received[:, :, :rank].astype(jnp.float32), axis=0).astype(jnp.bfloat16)
    far = jnp.einsum("kfr,kr->kf", cluster_basis, owned, preferred_element_type=jnp.float32)
    return finish(listed, edges, received, near, far, rank), damage


def solution(mesh):
    both = ("rows", "cols")
    in_specs = (
        P(both, None),
        P(both, None),
        P(both, None, None),
        P(both, None),
        P(both),
        P(both, None),
        P(both),
        P(both, None, None),
        P(both, None),
        P(both, None),
    )
    out_specs = (P(both, None), P(both, None))
    return jax.shard_map(local, mesh=mesh, in_specs=in_specs, out_specs=out_specs, check_vma=False)
```

profile of v0, /device:TPU:18, one launch (start us, length us, event | category | flops | bytes accessed | tf_op | source)
XLA Modules:
  0.0 36.0 jit_solution(5430934635873917480)
XLA Ops:
  0.6 0.0 copy-start
  2.2 1.0 %prepare.1 = (bf16[64,288]{1,0:T(8,128)(2,1)S(1)}, f32[64,64]{1,0:T(8,128)S(1)}, s32[8,128]{1,0:T(8,128)S(1)}) custom-call(s32[1]{0:T(128)S(6)} %copy.22.near_count_ref, s32[1]{0:T(128)S(6)} %copy.23.far_count_ref, f32[64,288]{1,0:T(8,128)} %disp_hbm.5, f32[64,288]{1,0:T(8,128)} %pos_hbm.3), custom_call_target="tpu_custom_call" | custom-call | flops 18432 | bytes 221184 | tf_op jit(solution)/shard_map/prepare/pallas_call | solution.py:122
  3.3 0.0 copy-done
  3.3 1.2 %fusion = f32[64,1,64]{2,1,0:T(1,128)S(1)} fusion(bf16[64,288,64]{1,2,0:T(8,128)(2,1)S(1)} %copy-done, bf16[64,288,1]{1,0,2:T(8,128)(2,1)S(1)} %bitcast.13), kind=kOutput, calls=%fused_computation.2 | convolution fusion | flops 2359296 | bytes 2412544 | tf_op jit(solution)/shard_map/kf,kfr->kr/dot_general | solution.py:708
  4.5 0.1 pad_maximum_fusion
  4.6 5.4 %all_gather.3.gathered_hbm = f32[256,128]{1,0:T(8,128)S(1)} all-gather(f32[64,128]{1,0:T(8,128)S(1)} %pad_maximum_fusion), channel_id=1, replica_groups=mesh['rows'=4,'cols'=8] {'rows'}, dimensions={0}, use_global_device_ids=true | all-gather | bytes 163840 | tf_op jit(solution)/shard_map/all_gather | solution.py:710
  10.0 6.2 %far_field.1 = (bf16[8,64,128]{2,1,0:T(8,128)(2,1)}, f32[64,288]{1,0:T(8,128)S(1)}, f32[64,96]{1,0:T(8,128)S(1)}, s32[8,256]{1,0:T(8,128)S(1)}, f32[64,96]{1,0:T(8,128)}) custom-call(s32[8,128]{1,0:T(8,128)S(1)} %get-tuple-element.12.counts_hbm, s32[2,1024]{1,0:T(2,128)} %bitcast.17, f32[256,128]{1,0:T(8,128)S(1)} %all_gather.3.gathered_hbm, ...), custom_call_target="tpu_custom_call" | custom-call | flops 8388608 | bytes 8388608 | tf_op jit(solution)/shard_map/far_field/pallas_call | solution.py:316
  16.2 5.1 %all-to-all-start = ((bf16[8,64,128]{2,1,0:T(8,128)(2,1)}), bf16[8,64,128]{2,1,0:T(8,128)(2,1)S(1)}, u32[]{:S(2)}, u32[]{:S(2)}) async-start(bf16[8,64,128]{2,1,0:T(8,128)(2,1)} %get-tuple-element.19), calls=%async_computation | async-start | bytes 262144 | tf_op jit(solution)/shard_map/all_to_all | solution.py:724
  21.4 11.9 %near_field.1 = (f32[64,288]{1,0:T(8,128)S(1)}, f32[4,288]{1,0:T(4,128)S(1)}) custom-call(s32[8,256]{1,0:T(8,128)S(1)} %get-tuple-element.15.list_hbm.rest_hbm, f32[64,288]{1,0:T(8,128)} %disp_hbm.5, f32[64,288]{1,0:T(8,128)S(1)} %get-tuple-element.16.pos_ref, f32[64,96]{1,0:T(8,128)S(1)} %get-tuple-element.17.hold_ref), custom_call_target="tpu_custom_call" | custom-call | flops 70778880 | bytes 442368 | tf_op jit(solution)/shard_map/near_field/pallas_call | solution.py:537
  33.2 0.0 all-to-all-done.received_ref
  33.3 0.6 %fusion.2 = f32[64,1,288]{2,1,0:T(1,128)S(1)} fusion(bf16[64,288,64]{1,2,0:T(8,128)(2,1)S(1)} %copy-done, bf16[64,64,1]{1,0,2:T(8,128)(2,1)S(1)} %bitcast.15), kind=kOutput, calls=%fused_computation.5 | convolution fusion | flops 2359296 | bytes 2441216 | tf_op jit(solution)/shard_map/kfr,kr->kf/dot_general | solution.py:727
  33.9 2.0 %finish.1 = f32[64,288]{1,0:T(8,128)} custom-call(s32[8,256]{1,0:T(8,128)S(1)} %get-tuple-element.15.list_hbm.rest_hbm, f32[4,288]{1,0:T(4,128)S(1)} %get-tuple-element.18.edge_ref, bf16[8,64,128]{2,1,0:T(8,128)(2,1)S(1)} %all-to-all-done.received_ref, f32[64,288]{1,0:T(8,128)S(1)} %get-tuple-element.20.near_ref, f32[64,288]{1,0:T(8,128)S(1)} %bitcast.12), custom_call_target="tpu_custom_call" | custom-call | flops 36864 | bytes 294912 | tf_op jit(solution)/shard_map/finish/pallas_call | solution.py:669
  (2 shorter events, 0.0 us)
Async XLA Ops:
  0.6 2.7 %copy-start = (bf16[64,288,64]{1,2,0:T(8,128)(2,1)S(1)}, bf16[64,288,64]{1,2,0:T(8,128)(2,1)}, u32[]{:S(2)}) copy-start(bf16[64,288,64]{1,2,0:T(8,128)(2,1)} %param.12) | copy-start | bytes 7077892
  16.2 17.0 %all-to-all-start = ((bf16[8,64,128]{2,1,0:T(8,128)(2,1)}), bf16[8,64,128]{2,1,0:T(8,128)(2,1)S(1)}, u32[]{:S(2)}, u32[]{:S(2)}) async-start(bf16[8,64,128]{2,1,0:T(8,128)(2,1)} %get-tuple-element.19), calls=%async_computation | async-start | bytes 262144 | tf_op jit(solution)/shard_map/all_to_all | solution.py:724
where the time goes:
time: 36.4 us; the launch traced here: 36 us
  Pallas kernels  21.2 us (58%)
  blocking collectives  5.42 us (15%)
  starting transfers between devices  5.11 us (14%)
  between operations  2.29 us (6%)
  matrix products  1.82 us (5%)
    pallas_call x1, Pallas kernels, near_field(): pl.pallas_call(near_kernel, out_shape=(jax.ShapeDtypeStruct((clusters, wi...  11.9 us
    pallas_call x1, Pallas kernels, far_field(): pl.pallas_call(functools.partial(far_kernel, segments=segments), out_shap...  6.24 us
    all_gather x1, blocking collectives, local(): gathered = lax.all_gather(payload, 'rows', axis=0, tiled=True)  5.42 us
    all_to_all x1, starting transfers between devices, local(): received = lax.all_to_all(partial, 'cols', split_axis=0, concat_axis=0)  5.11 us
    pallas_call x1, Pallas kernels, finish(): pl.pallas_call(functools.partial(finish_kernel, rank=rank), out_shape=jax...  2.04 us
    dot_general x1, matrix products, local(): jnp.einsum('kf,kfr->kr', disp_bf, cluster_basis, preferred_element_type=j...  1.18 us
    pallas_call x1, Pallas kernels, prepare(): pl.pallas_call(prepare_kernel, out_shape=(jax.ShapeDtypeStruct((clusters,...  1.04 us
  transfers between devices with their start and end apart: 1, of which 0 were waited for; matrix products, arithmetic and copies ran while one was open for 0% of the time, Pallas kernels for 33%

commit v1 on v0

--- a/solution.py
+++ b/solution.py
@@ -168,6 +168,7 @@
     column_scr,
     coeff_scr,
     place_scr,
+    both_scr,
     sum_scr,
     summed_scr,
     halo_scr,
@@ -203,14 +204,15 @@
         ),
     )
     fetch(0).start()
-    summed_scr[...] = jnp.zeros_like(summed_scr)
+    both_scr[...] = jnp.zeros_like(both_scr)
     inputs[0].wait()
     count = counts_ref[1, 0]
-    live = (count + FOLD - 1) // FOLD
-
-    @pl.when(live > 1)
-    def _():
-        fetch(1).start()
+    live = jnp.maximum((count + FOLD - 1) // FOLD, 1)
+    for t in range(1, slots // FOLD):
+
+        @pl.when(t < live)
+        def _(t=t):
+            fetch(t).start()
 
     inputs[1].wait()
     inputs[2].wait()
@@ -245,11 +247,6 @@
         start = pl.multiple_of(t * FOLD, FOLD)
         lanes = pl.ds(start, FOLD)
         fetch(t).wait()
-
-        @pl.when(t + 2 < live)
-        def _():
-            fetch(t + 2).start()
-
         coeff = coeff_scr[:, lanes]
         for r in range(rank):
             product = buffer[r, :, lanes].astype(jnp.float32) * coeff
@@ -269,13 +266,14 @@
         coupled = jnp.concatenate(parts, axis=1)
         high = coupled.astype(jnp.bfloat16)
         low = (coupled - high.astype(jnp.float32)).astype(jnp.bfloat16)
-        both = jnp.concatenate([high, low], axis=0)
-        summed_scr[...] += lax.dot_general(
-            place_scr[:, lanes], both, (((1,), (1,)), ((), ())), preferred_element_type=jnp.float32
-        )
+        both_scr[0:rank, lanes] = high
+        both_scr[rank : 2 * rank, lanes] = low
         return carry
 
     lax.fori_loop(0, live, multiply, 0)
+    summed_scr[...] = lax.dot_general(
+        place_scr[...], both_scr[...], (((1,), (1,)), ((), ())), preferred_element_type=jnp.float32
+    )
     damage_out.wait()
 
     i = lax.axis_index("rows")
@@ -337,6 +335,7 @@
             pltpu.VMEM((rows * clusters, LANES), jnp.bfloat16),
             pltpu.VMEM((rank, slots), jnp.float32),
             pltpu.VMEM((cols * clusters, slots), jnp.bfloat16),
+            pltpu.VMEM((2 * rank, slots), jnp.bfloat16),
             pltpu.VMEM((FOLD // LANES, rank * SUBLANES, LANES), jnp.float32),
             pltpu.VMEM((cols * clusters, LANES), jnp.float32),
             pltpu.VMEM((2, clusters, LANES), jnp.float32),

time: 36.4 us -> 36 us (0.989)
  the two profiles are of different devices: /device:TPU:18 before, /device:TPU:0 now
where the time goes in v1:
time: 36 us; the launch traced here: 36.1 us
  Pallas kernels  18.8 us (52%)
  starting transfers between devices  6.54 us (18%)
  blocking collectives  6.5 us (18%)
  between operations  2.29 us (6%)
  matrix products  1.82 us (5%)
    pallas_call x1, Pallas kernels, near_field(): pl.pallas_call(near_kernel, out_shape=(jax.ShapeDtypeStruct((clusters, wi...  11.2 us
    all_to_all x1, starting transfers between devices, local(): received = lax.all_to_all(partial, 'cols', split_axis=0, concat_axis=0)  6.54 us
    all_gather x1, blocking collectives, local(): gathered = lax.all_gather(payload, 'rows', axis=0, tiled=True)  6.5 us
    pallas_call x1, Pallas kernels, far_field(): pl.pallas_call(functools.partial(far_kernel, segments=segments), out_shap...  4.46 us
    pallas_call x1, Pallas kernels, finish(): pl.pallas_call(functools.partial(finish_kernel, rank=rank), out_shape=jax...  2.04 us
    dot_general x1, matrix products, local(): jnp.einsum('kf,kfr->kr', disp_bf, cluster_basis, preferred_element_type=j...  1.18 us
    pallas_call x1, Pallas kernels, prepare(): pl.pallas_call(prepare_kernel, out_shape=(jax.ShapeDtypeStruct((clusters,...  1.04 us
  transfers between devices with their start and end apart: 1, of which 0 were waited for; matrix products, arithmetic and copies ran while one was open for 0% of the time, Pallas kernels for 31%

profile of v1, /device:TPU:0, one launch (start us, length us, event | category | flops | bytes accessed | tf_op | source)
XLA Modules:
  0.0 36.1 jit_solution(17790393701018909345)
XLA Ops:
  0.6 0.0 copy-start
  2.2 1.0 %prepare.1 = (bf16[64,288]{1,0:T(8,128)(2,1)S(1)}, f32[64,64]{1,0:T(8,128)S(1)}, s32[8,128]{1,0:T(8,128)S(1)}) custom-call(s32[1]{0:T(128)S(6)} %copy.22.near_count_ref, s32[1]{0:T(128)S(6)} %copy.23.far_count_ref, f32[64,288]{1,0:T(8,128)} %disp_hbm.5, f32[64,288]{1,0:T(8,128)} %pos_hbm.3), custom_call_target="tpu_custom_call" | custom-call | flops 18432 | bytes 221184 | tf_op jit(solution)/shard_map/prepare/pallas_call | solution.py:122
  3.3 0.0 copy-done
  3.3 1.2 %fusion = f32[64,1,64]{2,1,0:T(1,128)S(1)} fusion(bf16[64,288,64]{1,2,0:T(8,128)(2,1)S(1)} %copy-done, bf16[64,288,1]{1,0,2:T(8,128)(2,1)S(1)} %bitcast.13), kind=kOutput, calls=%fused_computation.2 | convolution fusion | flops 2359296 | bytes 2412544 | tf_op jit(solution)/shard_map/kf,kfr->kr/dot_general | solution.py:707
  4.5 0.1 pad_maximum_fusion
  4.6 6.5 %all_gather.3.gathered_hbm = f32[256,128]{1,0:T(8,128)S(1)} all-gather(f32[64,128]{1,0:T(8,128)S(1)} %pad_maximum_fusion), channel_id=1, replica_groups=mesh['rows'=4,'cols'=8] {'rows'}, dimensions={0}, use_global_device_ids=true | all-gather | bytes 163840 | tf_op jit(solution)/shard_map/all_gather | solution.py:709
  11.1 4.5 %far_field.1 = (bf16[8,64,128]{2,1,0:T(8,128)(2,1)}, f32[64,288]{1,0:T(8,128)S(1)}, f32[64,96]{1,0:T(8,128)S(1)}, s32[8,256]{1,0:T(8,128)S(1)}, f32[64,96]{1,0:T(8,128)}) custom-call(s32[8,128]{1,0:T(8,128)S(1)} %get-tuple-element.12.counts_hbm, s32[2,1024]{1,0:T(2,128)} %bitcast.17, f32[256,128]{1,0:T(8,128)S(1)} %all_gather.3.gathered_hbm, ...), custom_call_target="tpu_custom_call" | custom-call | flops 8388608 | bytes 8388608 | tf_op jit(solution)/shard_map/far_field/pallas_call | solution.py:314
  15.5 6.5 %all-to-all-start = ((bf16[8,64,128]{2,1,0:T(8,128)(2,1)}), bf16[8,64,128]{2,1,0:T(8,128)(2,1)S(1)}, u32[]{:S(2)}, u32[]{:S(2)}) async-start(bf16[8,64,128]{2,1,0:T(8,128)(2,1)} %get-tuple-element.19), calls=%async_computation | async-start | bytes 262144 | tf_op jit(solution)/shard_map/all_to_all | solution.py:723
  22.1 11.2 %near_field.1 = (f32[64,288]{1,0:T(8,128)S(1)}, f32[4,288]{1,0:T(4,128)S(1)}) custom-call(s32[8,256]{1,0:T(8,128)S(1)} %get-tuple-element.15.list_hbm.rest_hbm, f32[64,288]{1,0:T(8,128)} %disp_hbm.5, f32[64,288]{1,0:T(8,128)S(1)} %get-tuple-element.16.pos_ref, f32[64,96]{1,0:T(8,128)S(1)} %get-tuple-element.17.hold_ref), custom_call_target="tpu_custom_call" | custom-call | flops 70778880 | bytes 442368 | tf_op jit(solution)/shard_map/near_field/pallas_call | solution.py:536
  33.3 0.0 all-to-all-done.received_ref
  33.4 0.6 %fusion.2 = f32[64,1,288]{2,1,0:T(1,128)S(1)} fusion(bf16[64,288,64]{1,2,0:T(8,128)(2,1)S(1)} %copy-done, bf16[64,64,1]{1,0,2:T(8,128)(2,1)S(1)} %bitcast.15), kind=kOutput, calls=%fused_computation.5 | convolution fusion | flops 2359296 | bytes 2441216 | tf_op jit(solution)/shard_map/kfr,kr->kf/dot_general | solution.py:726
  34.0 2.0 %finish.1 = f32[64,288]{1,0:T(8,128)} custom-call(s32[8,256]{1,0:T(8,128)S(1)} %get-tuple-element.15.list_hbm.rest_hbm, f32[4,288]{1,0:T(4,128)S(1)} %get-tuple-element.18.edge_ref, bf16[8,64,128]{2,1,0:T(8,128)(2,1)S(1)} %all-to-all-done.received_ref, f32[64,288]{1,0:T(8,128)S(1)} %get-tuple-element.20.near_ref, f32[64,288]{1,0:T(8,128)S(1)} %bitcast.12), custom_call_target="tpu_custom_call" | custom-call | flops 36864 | bytes 294912 | tf_op jit(solution)/shard_map/finish/pallas_call | solution.py:668
  (2 shorter events, 0.0 us)
Async XLA Ops:
  0.6 2.7 %copy-start = (bf16[64,288,64]{1,2,0:T(8,128)(2,1)S(1)}, bf16[64,288,64]{1,2,0:T(8,128)(2,1)}, u32[]{:S(2)}) copy-start(bf16[64,288,64]{1,2,0:T(8,128)(2,1)} %param.12) | copy-start | bytes 7077892
  15.5 17.8 %all-to-all-start = ((bf16[8,64,128]{2,1,0:T(8,128)(2,1)}), bf16[8,64,128]{2,1,0:T(8,128)(2,1)S(1)}, u32[]{:S(2)}, u32[]{:S(2)}) async-start(bf16[8,64,128]{2,1,0:T(8,128)(2,1)} %get-tuple-element.19), calls=%async_computation | async-start | bytes 262144 | tf_op jit(solution)/shard_map/all_to_all | solution.py:723

commit v2 on v1

--- a/solution.py
+++ b/solution.py
@@ -49,9 +49,13 @@
     far_count_ref,
     disp_hbm,
     pos_hbm,
+    near_pairs_hbm,
+    far_pairs_hbm,
     low_ref,
     halo_ref,
     counts_ref,
+    near_pairs_ref,
+    far_pairs_ref,
     disp_ref,
     pos_ref,
     sems,
@@ -59,7 +63,15 @@
     clusters, width = disp_ref.shape
     spare = halo_ref.shape[1]
     segments = split_rows(width, spare)
-    inputs = start_all(sems, ((disp_hbm, disp_ref), (pos_hbm, pos_ref)))
+    inputs = start_all(
+        sems,
+        (
+            (disp_hbm, disp_ref),
+            (pos_hbm, pos_ref),
+            (near_pairs_hbm, near_pairs_ref),
+            (far_pairs_hbm, far_pairs_ref),
+        ),
+    )
     halo_ref[...] = jnp.zeros_like(halo_ref)
     row = lax.broadcasted_iota(jnp.int32, counts_ref.shape, 0)
     counts_ref[...] = jnp.where(row == 0, near_count_ref[0], far_count_ref[0])
@@ -115,7 +127,7 @@
     list_ref[7:8, :] = jnp.zeros((1, slots), jnp.int32)
 
 
-def prepare(near_count, far_count, disp, pos, spare):
+def prepare(near_count, far_count, disp, pos, near_pairs, far_pairs, spare):
     clusters, width = disp.shape
     vmem = pl.BlockSpec(memory_space=pltpu.VMEM)
     smem = pl.BlockSpec(memory_space=pltpu.SMEM)
@@ -125,27 +137,29 @@
             jax.ShapeDtypeStruct((clusters, width), jnp.bfloat16),
             jax.ShapeDtypeStruct((clusters, spare), jnp.float32),
             jax.ShapeDtypeStruct((SUBLANES, LANES), jnp.int32),
-        ),
-        in_specs=[smem] * 2 + in_hbm(2),
-        out_specs=(vmem,) * 3,
+            jax.ShapeDtypeStruct(near_pairs.shape, near_pairs.dtype),
+            jax.ShapeDtypeStruct(far_pairs.shape, far_pairs.dtype),
+        ),
+        in_specs=[smem] * 2 + in_hbm(4),
+        out_specs=(vmem,) * 5,
         scratch_shapes=[
             pltpu.VMEM(disp.shape, disp.dtype),
             pltpu.VMEM(pos.shape, pos.dtype),
-            pltpu.SemaphoreType.DMA((2,)),
+            pltpu.SemaphoreType.DMA((4,)),
         ],
         compiler_params=pltpu.CompilerParams(vmem_limit_bytes=VMEM),
         cost_estimate=pl.CostEstimate(
             flops=clusters * width, bytes_accessed=12 * clusters * width, transcendentals=0
         ),
         name="prepare",
-    )(near_count, far_count, *pinned(disp, pos))
+    )(near_count, far_count, *pinned(disp, pos, near_pairs, far_pairs))
 
 
 def far_kernel(
     counts_hbm,
-    pairs_hbm,
+    pairs_ref,
     gathered_hbm,
-    near_pairs_hbm,
+    near_pairs_ref,
     pos_hbm,
     disp_hbm,
     intact_hbm,
@@ -157,9 +171,7 @@
     list_ref,
     damage_hbm,
     counts_ref,
-    pairs_ref,
     gathered_ref,
-    near_pairs_ref,
     disp_ref,
     intact_ref,
     stiff_ref,
@@ -194,9 +206,7 @@
         sems,
         (
             (counts_hbm, counts_ref),
-            (pairs_hbm, pairs_ref),
             (gathered_hbm, gathered_ref),
-            (near_pairs_hbm, near_pairs_ref),
             (pos_hbm, pos_ref),
             (disp_hbm, disp_ref),
             (intact_hbm, intact_ref),
@@ -215,7 +225,6 @@
             fetch(t).start()
 
     inputs[1].wait()
-    inputs[2].wait()
     column_scr[...] = gathered_ref[...].astype(jnp.bfloat16)
 
     index = lax.broadcasted_iota(jnp.int32, (sources, slots), 0)
@@ -229,9 +238,9 @@
     index = lax.broadcasted_iota(jnp.int32, (targets, slots), 0)
     place_scr[...] = jnp.where(index == wanted, 1.0, 0.0).astype(jnp.bfloat16)
 
-    for copy in inputs[3:]:
+    list_pairs(near_pairs_ref, counts_ref[0, 0], list_ref, clusters)
+    for copy in inputs[2:]:
         copy.wait()
-    list_pairs(near_pairs_ref, counts_ref[0, 0], list_ref, clusters)
     elems = damage_ref.shape[1]
     disp = [disp_ref[:, c * elems : (c + 1) * elems] for c in range(3)]
     separation = jnp.sqrt(1.0 + (disp[0] * disp[0] + disp[1] * disp[1] + disp[2] * disp[2]))
@@ -310,6 +319,7 @@
 ):
     rank, _, slots = blocks.shape
     rows = lax.axis_size("rows")
+    vmem = pl.BlockSpec(memory_space=pltpu.VMEM)
     clusters = gathered.shape[0] // rows
     return pl.pallas_call(
         functools.partial(far_kernel, segments=segments),
@@ -320,13 +330,11 @@
             jax.ShapeDtypeStruct((SUBLANES, near_pairs.shape[1]), jnp.int32),
             jax.ShapeDtypeStruct(stiffness.shape, jnp.float32),
         ),
-        in_specs=in_hbm(9),
-        out_specs=(pl.BlockSpec(memory_space=pltpu.VMEM),) * 4 + tuple(in_hbm(1)),
+        in_specs=in_hbm(1) + [vmem] + in_hbm(1) + [vmem] + in_hbm(5),
+        out_specs=(vmem,) * 4 + tuple(in_hbm(1)),
         scratch_shapes=[
             pltpu.SMEM(counts.shape, counts.dtype),
-            pltpu.VMEM(pairs.shape, pairs.dtype),
             pltpu.VMEM(gathered.shape, gathered.dtype),
-            pltpu.VMEM(near_pairs.shape, near_pairs.dtype),
             pltpu.VMEM(disp.shape, disp.dtype),
             pltpu.VMEM(intact.shape, intact.dtype),
             pltpu.VMEM(stiffness.shape, stiffness.dtype),
@@ -339,7 +347,7 @@
             pltpu.VMEM((FOLD // LANES, rank * SUBLANES, LANES), jnp.float32),
             pltpu.VMEM((cols * clusters, LANES), jnp.float32),
             pltpu.VMEM((2, clusters, LANES), jnp.float32),
-            pltpu.SemaphoreType.DMA((8,)),
+            pltpu.SemaphoreType.DMA((6,)),
             pltpu.SemaphoreType.DMA((slots // FOLD,)),
             pltpu.SemaphoreType.DMA(()),
         ],
@@ -352,9 +360,10 @@
         name="far_field",
     )(
         counts,
-        *pinned(pairs),
+        pairs,
         gathered,
-        *pinned(near_pairs, pos, disp, intact, stiffness, blocks),
+        near_pairs,
+        *pinned(pos, disp, intact, stiffness, blocks),
     )
 
 
@@ -423,12 +432,12 @@
 
 
 def turn_matrix():
-    shape = (PIECES * CHUNK, SUBLANES * LANES)
+    shape = (CHUNK, SUBLANES * LANES)
     column = lax.broadcasted_iota(jnp.int32, shape, 1)
     lane = column % LANES
     entry = (lane + (lane // CHUNK) * SUBLANES + column // LANES) % CHUNK
-    row = lax.broadcasted_iota(jnp.int32, shape, 0) % CHUNK
-    return jnp.where(entry == row, 1.0, 0.0).astype(jnp.bfloat16)
+    chosen = jnp.where(entry == lax.broadcasted_iota(jnp.int32, shape, 0), 1.0, 0.0)
+    return jnp.concatenate([chosen.astype(jnp.bfloat16)] * PIECES, axis=0)
 
 
 def exact_pieces(value):
@@ -703,15 +712,17 @@
     clusters, width, rank = cluster_basis.shape
     spare = LANES - rank
     segments = split_rows(width, spare)
-    disp_bf, halo, counts = prepare(near_count, far_count, displacement, positions, spare)
+    disp_bf, halo, counts, near_list, far_list = prepare(
+        near_count, far_count, displacement, positions, near_pairs.T, far_pairs.T, spare
+    )
     coeff = jnp.einsum("kf,kfr->kr", disp_bf, cluster_basis, preferred_element_type=jnp.float32)
     payload = jnp.concatenate([coeff, halo], axis=1)
     gathered = lax.all_gather(payload, "rows", axis=0, tiled=True)
     partial, pos, hold, listed, damage = far_field(
         counts,
-        far_pairs.T,
+        far_list,
         gathered,
-        near_pairs.T,
+        near_list,
         positions,
         displacement,
         intact,

time: 36 us -> 36.6 us (1.017)
  the two profiles are of different devices: /device:TPU:0 before, /device:TPU:1 now
where the time goes in v2:
time: 36.6 us; the launch traced here: 36.8 us
  Pallas kernels  20.2 us (55%)
  blocking collectives  6.39 us (17%)
  starting transfers between devices  5.9 us (16%)
  between operations  2.29 us (6%)
  matrix products  1.82 us (5%)
    pallas_call x1, Pallas kernels, near_field(): pl.pallas_call(near_kernel, out_shape=(jax.ShapeDtypeStruct((clusters, wi...  11.9 us
    all_gather x1, blocking collectives, local(): gathered = lax.all_gather(payload, 'rows', axis=0, tiled=True)  6.39 us
    all_to_all x1, starting transfers between devices, local(): received = lax.all_to_all(partial, 'cols', split_axis=0, concat_axis=0)  5.9 us
    pallas_call x1, Pallas kernels, far_field(): pl.pallas_call(functools.partial(far_kernel, segments=segments), out_shap...  5.08 us
    pallas_call x1, Pallas kernels, finish(): pl.pallas_call(functools.partial(finish_kernel, rank=rank), out_shape=jax...  2.2 us
    dot_general x1, matrix products, local(): jnp.einsum('kf,kfr->kr', disp_bf, cluster_basis, preferred_element_type=j...  1.18 us
    pallas_call x1, Pallas kernels, prepare(): pl.pallas_call(prepare_kernel, out_shape=(jax.ShapeDtypeStruct((clusters,...  1.06 us
  transfers between devices with their start and end apart: 1, of which 0 were waited for; matrix products, arithmetic and copies ran while one was open for 0% of the time, Pallas kernels for 32%

profile of v2, /device:TPU:1, one launch (start us, length us, event | category | flops | bytes accessed | tf_op | source)
XLA Modules:
  0.0 36.8 jit_solution(3051208232098419636)
XLA Ops:
  0.6 0.0 copy-start
  2.2 1.1 %prepare.1 = (bf16[64,288]{1,0:T(8,128)(2,1)S(1)}, f32[64,64]{1,0:T(8,128)S(1)}, s32[8,128]{1,0:T(8,128)S(1)}, s32[2,256]{1,0:T(2,128)S(1)}, s32[2,1024]{1,0:T(2,128)S(1)}) custom-call(s32[1]{0:T(128)S(6)} %copy.22.near_count_ref, s32[1]{0:T(128)S(6)} %copy.23.far_count_ref, f32[64,288]{1,0:T(8,128)} %disp_hbm.5, f32[64,288]{1,0:T(8,128)} %pos_hbm.3, ...), custom_call_target="tpu_custom_call" | custom-call | flops 18432 | bytes 221184 | tf_op jit(solution)/shard_map/prepare/pallas_call | solution.py:134
  3.3 0.0 copy-done
  3.3 1.2 %fusion = f32[64,1,64]{2,1,0:T(1,128)S(1)} fusion(bf16[64,288,64]{1,2,0:T(8,128)(2,1)S(1)} %copy-done, bf16[64,288,1]{1,0,2:T(8,128)(2,1)S(1)} %bitcast.13), kind=kOutput, calls=%fused_computation.2 | convolution fusion | flops 2359296 | bytes 2412544 | tf_op jit(solution)/shard_map/kf,kfr->kr/dot_general | solution.py:718
  4.5 0.1 pad_maximum_fusion
  4.6 6.4 %all_gather.3.gathered_hbm = f32[256,128]{1,0:T(8,128)S(1)} all-gather(f32[64,128]{1,0:T(8,128)S(1)} %pad_maximum_fusion), channel_id=1, replica_groups=mesh['rows'=4,'cols'=8] {'rows'}, dimensions={0}, use_global_device_ids=true | all-gather | bytes 163840 | tf_op jit(solution)/shard_map/all_gather | solution.py:720
  11.0 5.1 %far_field.1 = (bf16[8,64,128]{2,1,0:T(8,128)(2,1)}, f32[64,288]{1,0:T(8,128)S(1)}, f32[64,96]{1,0:T(8,128)S(1)}, s32[8,256]{1,0:T(8,128)S(1)}, f32[64,96]{1,0:T(8,128)}) custom-call(s32[8,128]{1,0:T(8,128)S(1)} %get-tuple-element.14.counts_hbm, s32[2,1024]{1,0:T(2,128)S(1)} %get-tuple-element.15.pairs_ref, f32[256,128]{1,0:T(8,128)S(1)} %all_gather.3.gathered_hbm, ...), custom_call_target="tpu_custom_call" | custom-call | flops 8388608 | bytes 8388608 | tf_op jit(solution)/shard_map/far_field/pallas_call | solution.py:324
  16.1 5.9 %all-to-all-start = ((bf16[8,64,128]{2,1,0:T(8,128)(2,1)}), bf16[8,64,128]{2,1,0:T(8,128)(2,1)S(1)}, u32[]{:S(2)}, u32[]{:S(2)}) async-start(bf16[8,64,128]{2,1,0:T(8,128)(2,1)} %get-tuple-element.23), calls=%async_computation | async-start | bytes 262144 | tf_op jit(solution)/shard_map/all_to_all | solution.py:734
  22.0 11.9 %near_field.1 = (f32[64,288]{1,0:T(8,128)S(1)}, f32[4,288]{1,0:T(4,128)S(1)}) custom-call(s32[8,256]{1,0:T(8,128)S(1)} %get-tuple-element.19.list_hbm.rest_hbm, f32[64,288]{1,0:T(8,128)} %disp_hbm.5, f32[64,288]{1,0:T(8,128)S(1)} %get-tuple-element.20.pos_ref, f32[64,96]{1,0:T(8,128)S(1)} %get-tuple-element.21.hold_ref), custom_call_target="tpu_custom_call" | custom-call | flops 70778880 | bytes 442368 | tf_op jit(solution)/shard_map/near_field/pallas_call | solution.py:545
  33.8 0.0 all-to-all-done.received_ref
  33.9 0.6 %fusion.2 = f32[64,1,288]{2,1,0:T(1,128)S(1)} fusion(bf16[64,288,64]{1,2,0:T(8,128)(2,1)S(1)} %copy-done, bf16[64,64,1]{1,0,2:T(8,128)(2,1)S(1)} %bitcast.15), kind=kOutput, calls=%fused_computation.5 | convolution fusion | flops 2359296 | bytes 2441216 | tf_op jit(solution)/shard_map/kfr,kr->kf/dot_general | solution.py:737
  34.6 2.2 %finish.1 = f32[64,288]{1,0:T(8,128)} custom-call(s32[8,256]{1,0:T(8,128)S(1)} %get-tuple-element.19.list_hbm.rest_hbm, f32[4,288]{1,0:T(4,128)S(1)} %get-tuple-element.22.edge_ref, bf16[8,64,128]{2,1,0:T(8,128)(2,1)S(1)} %all-to-all-done.received_ref, f32[64,288]{1,0:T(8,128)S(1)} %get-tuple-element.24.near_ref, f32[64,288]{1,0:T(8,128)S(1)} %bitcast.12), custom_call_target="tpu_custom_call" | custom-call | flops 36864 | bytes 294912 | tf_op jit(solution)/shard_map/finish/pallas_call | solution.py:677
  (2 shorter events, 0.0 us)
Async XLA Ops:
  0.6 2.7 %copy-start = (bf16[64,288,64]{1,2,0:T(8,128)(2,1)S(1)}, bf16[64,288,64]{1,2,0:T(8,128)(2,1)}, u32[]{:S(2)}) copy-start(bf16[64,288,64]{1,2,0:T(8,128)(2,1)} %param.12) | copy-start | bytes 7077892
  16.1 17.8 %all-to-all-start = ((bf16[8,64,128]{2,1,0:T(8,128)(2,1)}), bf16[8,64,128]{2,1,0:T(8,128)(2,1)S(1)}, u32[]{:S(2)}, u32[]{:S(2)}) async-start(bf16[8,64,128]{2,1,0:T(8,128)(2,1)} %get-tuple-element.23), calls=%async_computation | async-start | bytes 262144 | tf_op jit(solution)/shard_map/all_to_all | solution.py:734
